TPU v7x, 256 devices: a whole 4x4x8 slice. The times are simulated.
256 devices in a mesh: view: 16 (over z, core), span: 16 (over x, y).
Axes of the slice: x: 4, y: 4, z: 8, core: 2. Of those that a mesh axis runs over, the one named last changes fastest.
Arguments:
- tokens: bfloat16 [16, 4096, 1024], P('view', 'span'), may hold values from -6 to 6
- scan_order: int32 [16, 4096], P('view'), may hold values from 0 to 4095, as said below
- w_merge: bfloat16 [4096, 1024], replicated, may hold values from -0.09375 to 0.09375
- bias: bfloat16 [1024], replicated, may hold values from -4 to 4
- cotangent: bfloat16 [16, 1024, 1024], P('view', 'span'), may hold values from -6 to 6
Outputs:
- merged_out: bfloat16 [16, 1024, 1024], P('view', 'span')
- token_grad: bfloat16 [16, 4096, 1024], P('view', 'span')
- weight_grad: float32 [4096, 1024], P(('view', 'span'))
- bias_grad: float32 [1024], replicated
Inputs may be any that keep to these rules, and one draw needn't show every extreme that they name: `scan_order`: each row is a permutation of the raster indices of one view. Call tokens 256 * b to 256 * (b + 1) - 1 band b, and scan positions 256 * c to 256 * (c + 1) - 1 block c: every block holds at most 24 tokens of any band, and in every row each block holds exactly 24 tokens of some band.
All inputs are finite; a program needn't handle non-finite values.
Results may differ from a plain program's by a relative error of at most 0.001.
Values may be sent and summed in bfloat16 or wider, within the bound.
A program may use at most 128 MiB of HBM per device.

v0:
```python
import math

import jax
import jax.numpy as jnp
from jax import lax
from jax.sharding import PartitionSpec as P

COLS = 128


def body(tokens, scan_order, w_merge, bias, cotangent):
    spans = lax.axis_size("span")
    views = lax.axis_size("view")
    span_index = lax.axis_index("span")
    tok_dev = tokens.shape[1]
    width = tokens.shape[2]
    capacity = 3 * (tok_dev // spans) // 2
    rows_dev = tok_dev // COLS
    order_all = scan_order[0].reshape(spans, tok_dev)
    owners = order_all // tok_dev
    owner_hot = (owners[:, :, None] == jnp.arange(spans, dtype=jnp.int32)[None, None, :]).astype(
        jnp.int32
    )
    slot_rank = jnp.sum((jnp.cumsum(owner_hot, axis=1) - 1) * owner_hot, axis=2)
    dest_slots = owners * capacity + slot_rank
    my_slots = lax.dynamic_index_in_dim(dest_slots, span_index, 0, keepdims=False)
    outgoing = jnp.zeros((spans * capacity, width), jnp.bfloat16).at[my_slots].set(tokens[0])
    received = lax.all_to_all(
        outgoing.reshape(spans, capacity, width), "span", split_axis=0, concat_axis=0, tiled=True
    )
    arriving = owners == span_index
    source_slot = jnp.arange(spans, dtype=jnp.int32)[:, None] * capacity + slot_rank
    local_index = jnp.where(arriving, order_all - span_index * tok_dev, tok_dev)
    source_of = (
        jnp.zeros((tok_dev,), jnp.int32)
        .at[local_index.reshape(-1)]
        .set(source_slot.reshape(-1), mode="drop")
    )
    raster = received.reshape(spans * capacity, width)[source_of]
    merged = (
        raster.reshape(rows_dev // 2, 2, COLS // 2, 2, width)
        .transpose(0, 2, 1, 3, 4)
        .reshape(tok_dev // 4, 4 * width)
    )
    merged_out = (
        jnp.dot(merged, w_merge, preferred_element_type=jnp.float32) + bias.astype(jnp.float32)
    ).astype(jnp.bfloat16)
    grads = cotangent[0]
    grad_merged = lax.dot_general(
        grads, w_merge, (((1,), (1,)), ((), ())), preferred_element_type=jnp.float32
    ).astype(jnp.bfloat16)
    grad_raster = (
        grad_merged.reshape(rows_dev // 2, COLS // 2, 2, 2, width)
        .transpose(0, 2, 1, 3, 4)
        .reshape(tok_dev, width)
    )
    going_back = jnp.zeros((spans * capacity, width), jnp.bfloat16).at[source_of].set(grad_raster)
    returned = lax.all_to_all(
        going_back.reshape(spans, capacity, width), "span", split_axis=0, concat_axis=0, tiled=True
    )
    token_grad = returned.reshape(spans * capacity, width)[my_slots]
    weight_sum = lax.psum_scatter(
        lax.dot_general(
            merged, grads, (((0,), (0,)), ((), ())), preferred_element_type=jnp.float32
        ),
        ("view", "span"),
        scatter_dimension=0,
        tiled=True,
    )
    bias_total = lax.psum(jnp.sum(grads.astype(jnp.float32), axis=0), ("view", "span"))
    grad_scale = 1.0 / math.sqrt(views * spans * (tok_dev // 4))
    return (merged_out[None], token_grad[None], weight_sum * grad_scale, bias_total * grad_scale)


def solution(mesh):
    in_specs = (P("view", "span", None), P("view", None), P(), P(), P("view", "span", None))
    out_specs = (P("view", "span", None), P("view", "span", None), P(("view", "span"), None), P())
    return jax.shard_map(body, mesh=mesh, in_specs=in_specs, out_specs=out_specs, check_vma=False)
```

profile of v0, /device:TPU:0, one launch (start us, length us, event | category | flops | bytes accessed | tf_op | source)
XLA Modules:
  0.0 1363.6 jit_solution(8147675132378394235)
XLA Ops:
  7.2 0.8 and_select_fusion.1
  8.0 9.1 reduce-window.6
  17.3 0.3 copy.9
  17.6 0.5 broadcast.237
  18.1 1.4 reduce.3
  19.8 2.6 scatter_custom_fusion
  22.4 5.3 all-to-all-start
  27.7 0.8 compare_select_fusion
  28.6 15.5 %scatter_custom_fusion.1 = s32[256]{0:T(256)S(1)} fusion(s32[4096]{0:T(1024)S(1)} %bitcast.73, s32[4096]{0:T(1024)S(1)} %bitcast.74, s32[]{:T(128)} %constant.19.clone.1), kind=kCustom, calls=%fused_computation.59 | custom fusion | bytes 1028 | tf_op jit(solution)/shard_map/scatter | solution.py:37
  44.2 1.2 gather_fusion
  45.6 0.4 copy.20
  45.9 0.4 reshape.221
  46.3 8.1 fusion.10
  54.5 6.0 convolution_convert_fusion
  60.5 0.4 reshape.222
  60.9 0.4 copy.19
  61.5 2.6 scatter_custom_fusion.2
  64.1 7.2 all-to-all-start.1
  71.3 83.0 %psum.7 = f32[1024]{0:T(1024)S(1)} all-reduce(f32[1024]{0:T(1024)S(1)} %convert_reduce_fusion), channel_id=1, replica_groups=mesh['view'=16,'span'=16] {'view','span'}, use_global_device_ids=true, to_apply=%region_8.9 | all-reduce | flops 1024 | bytes 8192 | tf_op jit(solution)/shard_map/psum | solution.py:70
  154.4 0.6 broadcast_multiply_fusion.1
  155.0 2.0 gather_fusion.1
  156.9 5.6 fusion.1
  162.5 1192.8 %reduce-scatter.2.cloned.1.call-done = f32[16,1024]{1,0:T(8,128)} async-done(((f32[4096,1024]{1,0:T(8,128)}), f32[16,1024]{1,0:T(8,128)}) %reduce-scatter.2.cloned.1.call-update) | async-done | bytes 65552 | tf_op jit(solution)/shard_map/reduce_scatter | solution.py:62
  1355.3 1.5 broadcast_multiply_fusion
  (29 shorter events, 1.0 us)
Async XLA Ops:
  7.2 12.6 copy-start
  7.2 39.1 %copy-start.1 = (bf16[1,64,1024]{2,1,0:T(8,128)(2,1)S(1)}, bf16[1,64,1024]{2,1,0:T(8,128)(2,1)}, u32[]{:S(2)}) copy-start(bf16[1,64,1024]{2,1,0:T(8,128)(2,1)} %param.9) | copy-start | bytes 393220
  22.4 21.8 %all-to-all-start = ((bf16[16,24,1024]{2,1,0:T(8,128)(2,1)}), bf16[16,24,1024]{2,1,0:T(8,128)(2,1)S(1)}, u32[]{:S(2)}, u32[]{:S(2)}) async-start(bf16[16,24,1024]{2,1,0:T(8,128)(2,1)} %bitcast.6), calls=%async_computation | async-start | bytes 1572864 | tf_op jit(solution)/shard_map/all_to_all | solution.py:28
  27.7 1327.7 %reduce-scatter.2.cloned.1.call-start = ((), (), s32[]{:S(2)}) async-start(), calls=%async_computation.3 | async-start | bytes 16842752 | tf_op jit(solution)/shard_map/reduce_scatter | solution.py:62
  54.4 16.8 %copy-start.2 = (bf16[1024]{0:T(1024)(128)(2,1)S(1)}, bf16[1024]{0:T(1024)(128)(2,1)}, u32[]{:S(2)}) copy-start(bf16[1024]{0:T(1024)(128)(2,1)} %param.8) | copy-start | bytes 6148
  64.1 90.9 %all-to-all-start.1 = ((bf16[16,24,1024]{2,1,0:T(8,128)(2,1)}), bf16[16,24,1024]{2,1,0:T(8,128)(2,1)S(1)}, u32[]{:S(2)}, u32[]{:S(2)}) async-start(bf16[16,24,1024]{2,1,0:T(8,128)(2,1)} %bitcast.14), calls=%async_computation.1 | async-start | bytes 1572864 | tf_op jit(solution)/shard_map/all_to_all | solution.py:58
Sparse Core Ops, SparseCore 0:
  54.6 1300.7 reduce-scatter.1
where the time goes:
time: 1360 us
  waiting for transfers between devices  1190 us (88%)
  blocking collectives  83 us (6%)
  local copies, waits for them, and re-layouts  26.7 us (2%)
  matrix products  19.8 us (1%)
  other arithmetic  14.6 us (1%)
  between operations  14.3 us (1%)
    reduce_scatter x1, waiting for transfers between devices, body(): lax.psum_scatter(lax.dot_general(merged, grads, (((0,), (0,)), ((), ())),...  1190 us
    psum x1, blocking collectives, body(): lax.psum(jnp.sum(grads.astype(jnp.float32), axis=0), ('view', 'span'))  83 us
  transfers between devices with their start and end apart: 3, of which 1 were waited for; matrix products, arithmetic and copies ran while one was open for 3% of the time, Pallas kernels for 0%

commit v1 on v0

v1 whole, which is shorter than its diff:
```python
import functools
import math

import jax
import jax.numpy as jnp
from jax import lax
from jax.experimental import pallas as pl
from jax.experimental.pallas import tpu as pltpu
from jax.sharding import PartitionSpec as P

MESH = pl.DeviceIdType.MESH
F32 = jnp.float32
BF16 = jnp.bfloat16
NN = (((1,), (0,)), ((), ()))
NT = (((1,), (1,)), ((), ()))
TN = (((0,), (0,)), ((), ()))


def dot(a, b, dims=NN):
    return lax.dot_general(a, b, dims, preferred_element_type=F32)


def one_hot(hit):
    return jnp.where(hit, 1.0, 0.0).astype(BF16)


def kernel(
    views,
    spans,
    cols,
    scale,
    tokens_ref,
    order_ref,
    w_hbm,
    bias_ref,
    cot_ref,
    merged_out_ref,
    token_grad_ref,
    weight_grad_ref,
    bias_grad_ref,
    w_ref,
    out_ref,
    recv_ref,
    back_ref,
    ret_ref,
    pick_ref,
    place_ref,
    rank_ref,
    code_ref,
    merged_ref,
    grad_ref,
    blocks_ref,
    cot_a,
    cot_b,
    half_send,
    half_own,
    half_recv,
    final_ref,
    view_bias,
    w_sem,
    tok_send,
    tok_recv,
    back_send,
    back_recv,
    blk_send,
    blk_recv,
    one_send,
    one_recv,
    two_send,
    two_recv,
    bias_send,
    bias_recv,
    pair_send,
    pair_recv,
    fin_send,
    fin_recv,
):
    v = lax.axis_index("view")
    s = lax.axis_index("span")
    core = lax.rem(v, 2)
    z = v // 2
    side = 4
    x, y = s // side, lax.rem(s, side)
    tok = tokens_ref.shape[1]
    dm = tokens_ref.shape[2]
    half = dm // 2
    mt = tok // 4
    cap = 3 * (tok // spans) // 2
    slot = 2 * cap
    nz = views // 2
    part = final_ref.shape[1]
    width = blocks_ref.shape[2]
    hw = width // 2

    t_in = lax.rem(v * spans + s, views)
    own_span = (v * spans + s) // views
    own_core = t_in // nz

    def source(k):
        return k * 2 + own_core, own_span

    def target(j):
        r = s * views + core * nz + j
        return r // spans, lax.rem(r, spans)

    barrier = pltpu.get_barrier_semaphore()

    @pl.loop(1, spans)
    def _(i):
        pl.semaphore_signal(barrier, inc=1, device_id=(v, s ^ i), device_id_type=MESH)

    @pl.loop(1, views)
    def _(i):
        pl.semaphore_signal(barrier, inc=1, device_id=(v ^ i, s), device_id_type=MESH)

    @pl.loop(0, nz)
    def _(k):
        tv, ts = source(k)

        @pl.when(jnp.logical_or(tv != v, ts != s))
        def _():
            pl.semaphore_signal(barrier, inc=1, device_id=(tv, ts), device_id_type=MESH)

    w_copy = pltpu.make_async_copy(w_hbm, w_ref, w_sem)
    w_copy.start()

    before = one_hot(
        lax.broadcasted_iota(jnp.int32, (tok, tok), 0)
        < lax.broadcasted_iota(jnp.int32, (tok, tok), 1)
    )
    mine = order_ref[0:1, pl.ds(pl.multiple_of(s * tok, tok), tok)]
    owner = lax.shift_right_logical(mine, int(math.log2(tok)))
    hot = jnp.where(lax.broadcasted_iota(jnp.int32, (spans, tok), 0) == owner, 1.0, 0.0)
    rank = jnp.sum(dot(hot.astype(BF16), before) * hot, axis=0, keepdims=True).astype(jnp.int32)
    first = owner * slot + rank
    slots = jnp.concatenate([first, first + cap], axis=1)

    cot = cot_ref[0]
    cot_a[x, y] = cot[:, :half]
    cot_b[x, y] = cot[:, half:]

    group = spans // 4

    @pl.loop(0, 4)
    def _(t):
        rows = group * slot
        pick = one_hot(lax.broadcasted_iota(jnp.int32, (rows, 2 * tok), 0) + t * rows == slots)
        pick_ref[pl.ds(pl.multiple_of(t * rows, rows), rows), :] = pick
        sent = dot(pick[:, :tok], tokens_ref[0, :, :half]) + dot(
            pick[:, tok:], tokens_ref[0, :, half:]
        )
        out_ref[pl.ds(t * group, group)] = sent.astype(BF16).reshape(group, slot, half)

    recv_ref[s] = out_ref[s]

    waits = (spans - 1) + (views - 1) + nz
    same = jnp.logical_and(own_span == s, own_core == core)
    pl.semaphore_wait(barrier, jnp.where(same, waits - 1, waits))

    def swap(src, dst, send, recv, i):
        return pltpu.make_async_remote_copy(
            src_ref=src,
            dst_ref=dst,
            send_sem=send.at[i],
            recv_sem=recv.at[i],
            device_id=(v, s ^ i),
            device_id_type=MESH,
        )

    def tok_copy(i):
        return swap(out_ref.at[s ^ i], recv_ref.at[s], tok_send, tok_recv, i)

    def back_copy(i):
        return swap(back_ref.at[s ^ i], ret_ref.at[s], back_send, back_recv, i)

    def blk_copy(i):
        d = s ^ i
        src = merged_ref.at[:, pl.ds(pl.multiple_of(d * width, width), width)]
        return swap(src, blocks_ref.at[s], blk_send, blk_recv, i)

    def one_y(i):
        return pltpu.make_async_remote_copy(
            src_ref=cot_a.at[x, y],
            dst_ref=cot_a.at[x, y],
            send_sem=one_send.at[i],
            recv_sem=one_recv.at[i],
            device_id=(v, s ^ i),
            device_id_type=MESH,
        )

    def one_x(i):
        return pltpu.make_async_remote_copy(
            src_ref=cot_b.at[x, y],
            dst_ref=cot_b.at[x, y],
            send_sem=one_send.at[side + i],
            recv_sem=one_recv.at[side + i],
            device_id=(v, s ^ (i * side)),
            device_id_type=MESH,
        )

    def two_x(i):
        return pltpu.make_async_remote_copy(
            src_ref=cot_a.at[x],
            dst_ref=cot_a.at[x],
            send_sem=two_send.at[i],
            recv_sem=two_recv.at[i],
            device_id=(v, s ^ (i * side)),
            device_id_type=MESH,
        )

    def two_y(i):
        return pltpu.make_async_remote_copy(
            src_ref=cot_b.at[:, y],
            dst_ref=cot_b.at[:, y],
            send_sem=two_send.at[side + i],
            recv_sem=two_recv.at[side + i],
            device_id=(v, s ^ i),
            device_id_type=MESH,
        )

    def bias_copy(i):
        return pltpu.make_async_remote_copy(
            src_ref=view_bias.at[v],
            dst_ref=view_bias.at[v],
            send_sem=bias_send.at[i],
            recv_sem=bias_recv.at[i],
            device_id=(v ^ i, s),
            device_id_type=MESH,
        )

    pair = pltpu.make_async_remote_copy(
        src_ref=half_send,
        dst_ref=half_recv,
        send_sem=pair_send.at[0],
        recv_sem=pair_recv.at[0],
        device_id=(v ^ 1, s),
        device_id_type=MESH,
    )

    def fin_copy(j):
        tv, ts = target(j)
        return pltpu.make_async_remote_copy(
            src_ref=half_own.at[pl.ds(pl.multiple_of(j * part, part), part), :],
            dst_ref=final_ref.at[z],
            send_sem=fin_send.at[j],
            recv_sem=fin_recv.at[z],
            device_id=(tv, ts),
            device_id_type=MESH,
        )

    def fin_arrival(k):
        return pltpu.make_async_remote_copy(
            src_ref=half_own.at[pl.ds(0, part), :],
            dst_ref=final_ref.at[k],
            send_sem=fin_send.at[0],
            recv_sem=fin_recv.at[k],
            device_id=(v ^ 1, s),
            device_id_type=MESH,
        )

    @pl.loop(1, spans)
    def _(i):
        tok_copy(i).start()

    @pl.loop(1, side)
    def _(i):
        one_y(i).start()
        one_x(i).start()

    order = jnp.concatenate([order_ref[0:1, c * tok : (c + 1) * tok] for c in range(spans)], axis=0)
    arriving = lax.shift_right_logical(order, int(math.log2(tok))) == s
    arrive = jnp.where(arriving, 1.0, 0.0)
    rank_in = dot(arrive.astype(BF16), before)
    rank_ref[...] = jnp.where(arriving, rank_in, -1.0)
    local = lax.rem(order, tok)
    col = lax.rem(local, cols)
    quadrant = (local // cols) * 2 + lax.rem(col, 2)
    code_ref[...] = jnp.where(arriving, quadrant * mt + col // 2 + 1, 0).astype(F32)

    @pl.loop(0, spans)
    def _(c):
        rk = rank_ref[pl.ds(c, 1), :]
        cd = code_ref[pl.ds(c, 1), :]
        row = lax.broadcasted_iota(jnp.int32, (slot, tok), 0)
        k = jnp.where(row >= cap, row - cap, row).astype(F32)
        to = jnp.sum(jnp.where(rk == k, cd, 0.0), axis=1, keepdims=True).astype(jnp.int32)
        row = lax.broadcasted_iota(jnp.int32, (slot, 2 * tok), 0)
        lane = lax.broadcasted_iota(jnp.int32, (slot, 2 * tok), 1)
        wanted = jnp.where(row >= cap, lane - tok, lane) + 1
        wanted = jnp.where(wanted > tok, 0, wanted)
        place_ref[pl.ds(pl.multiple_of(c * slot, slot), slot), :] = one_hot(
            jnp.logical_and(to == wanted, wanted > 0)
        )

    @pl.loop(1, side)
    def _(i):
        one_y(i).wait_recv()
        one_x(i).wait_recv()

    @pl.loop(1, side)
    def _(i):
        two_x(i).start()
        two_y(i).start()

    w_copy.wait()

    @pl.loop(0, 8)
    def _(t):
        q, h = t // 2, lax.rem(t, 2)
        rows = w_ref[pl.ds(pl.multiple_of(t * half, half), half), :]
        g = dot(cot_ref[0], rows, NT).astype(BF16)
        grad_ref[pl.ds(pl.multiple_of(h * tok + q * mt, mt), mt), :] = g

    @pl.loop(0, 4)
    def _(t):
        rows = group * slot
        place = place_ref[pl.ds(pl.multiple_of(t * rows, rows), rows), :]
        back = dot(place, grad_ref[...]).astype(BF16)
        back_ref[pl.ds(t * group, group)] = back.reshape(group, slot, half)

    ret_ref[s] = back_ref[s]

    @pl.loop(1, spans)
    def _(i):
        tok_copy(i).wait_recv()

    arrived = recv_ref[...].reshape(spans * slot, half)
    for t in range(4):
        block = dot(place_ref[:, t * 2 * mt : (t + 1) * 2 * mt], arrived, TN).astype(BF16)
        h, q = t // 2, 2 * (t % 2)
        merged_ref[:, q * dm + h * half : q * dm + (h + 1) * half] = block[:mt]
        merged_ref[:, (q + 1) * dm + h * half : (q + 1) * dm + (h + 1) * half] = block[mt:]

    blocks_ref[s] = merged_ref[:, pl.ds(pl.multiple_of(s * width, width), width)]

    @pl.loop(1, spans)
    def _(i):
        blk_copy(i).start()

    @pl.loop(1, spans)
    def _(i):
        back_copy(i).start()

    @pl.loop(0, 4)
    def _(t):
        at = pl.ds(pl.multiple_of(t * 256, 256), 256)
        o = dot(merged_ref[...], w_ref[:, at]) + bias_ref[0:1, at].astype(F32)
        merged_out_ref[0, :, at] = o.astype(BF16)

    @pl.loop(1, side)
    def _(i):
        two_x(i).wait_recv()
        two_y(i).wait_recv()

    cots_a = cot_a[...].reshape(spans * mt, half)
    cots_b = cot_b[...].reshape(spans * mt, half)
    ones = jnp.ones((8, spans * mt), BF16)
    sum_a = dot(ones, cots_a)
    sum_b = dot(ones, cots_b)
    lanes = 128
    for i in range(half // lanes):
        view_bias[v, i : i + 1, :] = sum_a[0:1, i * lanes : (i + 1) * lanes]
        view_bias[v, half // lanes + i : half // lanes + i + 1, :] = sum_b[
            0:1, i * lanes : (i + 1) * lanes
        ]

    @pl.loop(1, views)
    def _(i):
        bias_copy(i).start()

    @pl.loop(1, spans)
    def _(i):
        blk_copy(i).wait_recv()

    def product(h, to):
        lhs = blocks_ref[:, :, pl.ds(pl.multiple_of(h * hw, hw), hw)].reshape(spans * mt, hw)
        to[:, :half] = dot(lhs, cot_a[...].reshape(spans * mt, half), TN)
        to[:, half:] = dot(lhs, cot_b[...].reshape(spans * mt, half), TN)

    product(1 - core, half_send)
    pair.start()
    product(core, half_own)
    pair.wait_recv()
    half_own[...] += half_recv[...]

    @pl.loop(0, nz)
    def _(j):
        tv, ts = target(j)
        here = jnp.logical_and(tv == v, ts == s)

        @pl.when(jnp.logical_not(here))
        def _():
            fin_copy(j).start()

        @pl.when(here)
        def _():
            final_ref[z] = half_own[pl.ds(pl.multiple_of(j * part, part), part), :]

    @pl.loop(1, spans)
    def _(i):
        back_copy(i).wait_recv()

    returned = ret_ref[...].reshape(spans * slot, half)
    for t in range(2):
        g = dot(pick_ref[:, t * tok : (t + 1) * tok], returned, TN)
        token_grad_ref[0, :, t * half : (t + 1) * half] = g.astype(BF16)

    @pl.loop(1, views)
    def _(i):
        bias_copy(i).wait_recv()

    bias_grad_ref[...] = jnp.sum(view_bias[...], axis=0) * scale

    @pl.loop(0, nz)
    def _(k):
        tv, ts = source(k)

        @pl.when(jnp.logical_or(tv != v, ts != s))
        def _():
            fin_arrival(k).wait_recv()

    weight_grad_ref[...] = jnp.sum(final_ref[...], axis=0) * scale

    @pl.loop(1, spans)
    def _(i):
        tok_copy(i).wait_send()
        blk_copy(i).wait_send()
        back_copy(i).wait_send()

    @pl.loop(1, side)
    def _(i):
        one_y(i).wait_send()
        one_x(i).wait_send()
        two_x(i).wait_send()
        two_y(i).wait_send()

    @pl.loop(1, views)
    def _(i):
        bias_copy(i).wait_send()

    pair.wait_send()

    @pl.loop(0, nz)
    def _(j):
        tv, ts = target(j)

        @pl.when(jnp.logical_or(tv != v, ts != s))
        def _():
            fin_copy(j).wait_send()


def body(views, spans, tokens, scan_order, w_merge, bias, cotangent):
    tok, dm = tokens.shape[1:]
    merge_in, do = w_merge.shape
    mt = tok // 4
    half = dm // 2
    slot = 3 * (tok // spans)
    width = merge_in // spans
    part = merge_in // (views * spans)
    side = 4
    scale = 1.0 / math.sqrt(views * spans * mt)
    vmem = pl.BlockSpec(memory_space=pltpu.VMEM)
    dma = pltpu.SemaphoreType.DMA
    merged_out, token_grad, weight_grad, bias_grad = pl.pallas_call(
        functools.partial(kernel, views, spans, 128, scale),
        out_shape=(
            jax.ShapeDtypeStruct((1, mt, do), BF16),
            jax.ShapeDtypeStruct((1, tok, dm), BF16),
            jax.ShapeDtypeStruct((part, do), F32),
            jax.ShapeDtypeStruct((do // 128, 128), F32),
        ),
        in_specs=[vmem, vmem, pl.BlockSpec(memory_space=pl.ANY), vmem, vmem],
        out_specs=(vmem, vmem, vmem, vmem),
        scratch_shapes=[
            pltpu.VMEM((merge_in, do), BF16),
            pltpu.VMEM((spans, slot, half), BF16),
            pltpu.VMEM((spans, slot, half), BF16),
            pltpu.VMEM((spans, slot, half), BF16),
            pltpu.VMEM((spans, slot, half), BF16),
            pltpu.VMEM((spans * slot, 2 * tok), BF16),
            pltpu.VMEM((spans * slot, 2 * tok), BF16),
            pltpu.VMEM((spans, tok), F32),
            pltpu.VMEM((spans, tok), F32),
            pltpu.VMEM((mt, merge_in), BF16),
            pltpu.VMEM((2 * tok, half), BF16),
            pltpu.VMEM((spans, mt, width), BF16),
            pltpu.VMEM((side, side, mt, half), BF16),
            pltpu.VMEM((side, side, mt, half), BF16),
            pltpu.VMEM((width // 2, do), F32),
            pltpu.VMEM((width // 2, do), F32),
            pltpu.VMEM((width // 2, do), F32),
            pltpu.VMEM((views // 2, part, do), F32),
            pltpu.VMEM((views, do // 128, 128), F32),
            dma,
            dma((spans,)),
            dma((spans,)),
            dma((spans,)),
            dma((spans,)),
            dma((spans,)),
            dma((spans,)),
            dma((2 * side,)),
            dma((2 * side,)),
            dma((2 * side,)),
            dma((2 * side,)),
            dma((views,)),
            dma((views,)),
            dma((1,)),
            dma((1,)),
            dma((views // 2,)),
            dma((views // 2,)),
        ],
        compiler_params=pltpu.CompilerParams(
            collective_id=0, has_side_effects=True, vmem_limit_bytes=48 * 2**20
        ),
    )(tokens, scan_order, w_merge, bias.reshape(1, do), cotangent)
    return merged_out, token_grad, weight_grad, bias_grad.reshape(do)


def solution(mesh):
    in_specs = (P("view", "span", None), P("view", None), P(), P(), P("view", "span", None))
    out_specs = (P("view", "span", None), P("view", "span", None), P(("view", "span"), None), P())
    return jax.shard_map(
        functools.partial(body, mesh.shape["view"], mesh.shape["span"]),
        mesh=mesh,
        in_specs=in_specs,
        out_specs=out_specs,
        check_vma=False,
    )
```

time: 1360 us -> 107 us (0.08)
  the two profiles are of different devices: /device:TPU:0 before, /device:TPU:1 now
where the time goes in v1:
time: 107 us
  Pallas kernels  100 us (93%)
  local copies, waits for them, and re-layouts  6.02 us (6%)
    pallas_call x1, Pallas kernels, body(): pl.pallas_call(functools.partial(kernel, views, spans, 128, scale), out_s...  100 us
    unnamed x10, local copies, waits for them, and re-layouts  5.33 us

profile of v1, /device:TPU:1, one launch (start us, length us, event | category | flops | bytes accessed | tf_op | source)
XLA Modules:
  0.0 106.7 jit_solution(737761566538068379)
XLA Ops:
  0.6 0.7 reshape.14.bias_ref
  1.3 0.0 copy-start
  1.3 1.0 copy-done
  2.4 0.0 copy-start.1
  2.4 0.9 copy-done.1
  3.3 0.0 copy-start.2
  3.3 0.7 copy-done.2
  4.0 100.1 %shard_map.84 = (bf16[1,64,1024]{2,1,0:T(8,128)(2,1)S(1)}, bf16[1,256,1024]{2,1,0:T(8,128)(2,1)S(1)}, f32[16,1024]{1,0:T(8,128)S(1)}, f32[8,128]{1,0:T(8,128)S(1)}) custom-call(bf16[1,256,1024]{2,1,0:T(8,128)(2,1)S(1)} %copy-done, s32[1,4096]{1,0:T(1,128)S(1)} %copy-done.2, bf16[4096,1024]{1,0:T(8,128)(2,1)} %w_hbm.1, bf16[1,1024]{1,0:T(2,128)(2,1)S(1)} %reshape.14.bias_ref, ...), custom_call_target="tpu_custom_call" | custom-call | tf_op jit(solution)/shard_map/pallas_call | solution.py:464
  104.1 0.7 copy.13
  104.7 0.8 copy.14
  105.5 0.6 copy.15
  106.1 0.6 copy.16
Async XLA Ops:
  1.3 1.0 copy-start
  2.4 0.9 copy-start.1
  3.3 0.7 copy-start.2

commit v2 on v1

v2 whole, which is shorter than its diff:
```python
import functools
import math

import jax
import jax.numpy as jnp
from jax import lax
from jax.experimental import pallas as pl
from jax.experimental.pallas import tpu as pltpu
from jax.sharding import PartitionSpec as P

MESH = pl.DeviceIdType.MESH
F32 = jnp.float32
BF16 = jnp.bfloat16
NN = (((1,), (0,)), ((), ()))
NT = (((1,), (1,)), ((), ()))
TN = (((0,), (0,)), ((), ()))


def dot(a, b, dims=NN):
    return lax.dot_general(a, b, dims, preferred_element_type=F32)


def one_hot(hit):
    return jnp.where(hit, 1.0, 0.0).astype(BF16)


def kernel(
    views,
    spans,
    cols,
    scale,
    tokens_ref,
    order_ref,
    w_hbm,
    bias_ref,
    cot_ref,
    merged_out_ref,
    token_grad_ref,
    weight_grad_ref,
    bias_grad_ref,
    w_ref,
    out_ref,
    recv_ref,
    back_ref,
    ret_ref,
    pick_ref,
    place_ref,
    rank_ref,
    code_ref,
    merged_ref,
    grad_ref,
    blocks_ref,
    cot_all,
    prod_a,
    prod_b,
    in_a,
    in_b,
    part_a,
    part_b,
    last_a,
    last_b,
    span_bias,
    w_sem,
    tok_send,
    tok_recv,
    back_send,
    back_recv,
    blk_send,
    blk_recv,
    ring_send,
    ring_recv,
    share_send,
    share_recv,
    bias_send,
    bias_recv,
    sum_send,
    sum_recv,
    last_send,
    last_recv,
):
    v = lax.axis_index("view")
    s = lax.axis_index("span")
    core = lax.rem(v, 2)
    z = v // 2
    nz = views // 2
    steps = nz // 2
    side = 4
    x, y = s // side, lax.rem(s, side)
    tok = tokens_ref.shape[1]
    dm = tokens_ref.shape[2]
    half = dm // 2
    quarter = dm // 4
    mt = tok // 4
    cap = 3 * (tok // spans) // 2
    slot = 2 * cap
    width = blocks_ref.shape[2]
    groups = dm // width

    barrier = pltpu.get_barrier_semaphore()

    @pl.loop(1, spans)
    def _(i):
        pl.semaphore_signal(barrier, inc=1, device_id=(v, s ^ i), device_id_type=MESH)

    @pl.loop(1, views)
    def _(i):
        pl.semaphore_signal(barrier, inc=1, device_id=(v ^ i, s), device_id_type=MESH)

    w_copy = pltpu.make_async_copy(w_hbm, w_ref, w_sem)
    w_copy.start()

    def remote(src, dst, send, recv, device):
        return pltpu.make_async_remote_copy(
            src_ref=src,
            dst_ref=dst,
            send_sem=send,
            recv_sem=recv,
            device_id=device,
            device_id_type=MESH,
        )

    def tok_copy(h, i):
        at = h * spans + i
        return remote(
            out_ref.at[h, s ^ i], recv_ref.at[h, s], tok_send.at[at], tok_recv.at[at], (v, s ^ i)
        )

    def back_copy(i):
        return remote(
            back_ref.at[s ^ i], ret_ref.at[s], back_send.at[i], back_recv.at[i], (v, s ^ i)
        )

    def blk_copy(d):
        i = d ^ v
        src = merged_ref.at[:, pl.ds(pl.multiple_of(d * width, width), width)]
        return remote(src, blocks_ref.at[v], blk_send.at[i], blk_recv.at[i], (d, s))

    def near(k):
        return lax.rem(z + 2 * nz - k, nz)

    def ring_copy(way, k):
        held = near(k - 1) if way == 0 else near(1 - k)
        to = near(-1) if way == 0 else near(1)
        ref = cot_all.at[held, core]
        if k == steps:
            ref = ref.at[:, way * half : (way + 1) * half]
        at = way * (steps + 1) + k
        return remote(ref, ref, ring_send.at[at], ring_recv.at[at], (to * 2 + core, s))

    def share_copy(k):
        ref = cot_all.at[near(k), core]
        return remote(ref, ref, share_send.at[k], share_recv.at[k], (v ^ 1, s))

    def bias_copy(i):
        ref = span_bias.at[s]
        return remote(ref, ref, bias_send.at[i], bias_recv.at[i], (v, s ^ i))

    def sum_y(i):
        return remote(prod_a.at[:, y ^ i], in_a.at[y], sum_send.at[i], sum_recv.at[i], (v, s ^ i))

    def sum_x(i):
        at = side + i
        return remote(
            prod_b.at[x ^ i], in_b.at[x], sum_send.at[at], sum_recv.at[at], (v, s ^ (i * side))
        )

    def last_x(i):
        return remote(
            part_a.at[x ^ i], last_a.at[x], last_send.at[i], last_recv.at[i], (v, s ^ (i * side))
        )

    def last_y(i):
        at = side + i
        return remote(
            part_b.at[y ^ i], last_b.at[y], last_send.at[at], last_recv.at[at], (v, s ^ i)
        )

    before = one_hot(
        lax.broadcasted_iota(jnp.int32, (tok, tok), 0)
        < lax.broadcasted_iota(jnp.int32, (tok, tok), 1)
    )
    bits = int(math.log2(tok))
    mine = order_ref[0:1, pl.ds(pl.multiple_of(s * tok, tok), tok)]
    owner = lax.shift_right_logical(mine, bits)
    hot = jnp.where(lax.broadcasted_iota(jnp.int32, (spans, tok), 0) == owner, 1.0, 0.0)
    rank = jnp.sum(dot(hot.astype(BF16), before) * hot, axis=0, keepdims=True).astype(jnp.int32)
    first = owner * slot + rank
    slots = jnp.concatenate([first, first + cap], axis=1)

    cot_all[z, core] = cot_ref[0]
    group = spans // 4
    rows = group * slot

    def fill(h):
        @pl.loop(0, 4)
        def _(t):
            at = pl.ds(pl.multiple_of(t * rows, rows), rows)
            if h == 0:
                pick_ref[at, :] = one_hot(
                    lax.broadcasted_iota(jnp.int32, (rows, 2 * tok), 0) + t * rows == slots
                )
            c = h * half
            sent = dot(pick_ref[at, :tok], tokens_ref[0, :, c : c + quarter]) + dot(
                pick_ref[at, tok:], tokens_ref[0, :, c + quarter : c + half]
            )
            out_ref[h, pl.ds(t * group, group)] = sent.astype(BF16).reshape(group, slot, quarter)

        recv_ref[h, s] = out_ref[h, s]

    fill(0)
    pl.semaphore_wait(barrier, spans + views - 2)
    ring_copy(0, 1).start()
    ring_copy(1, 1).start()

    @pl.loop(1, spans)
    def _(i):
        tok_copy(0, i).start()

    share_copy(0).start()
    fill(1)

    @pl.loop(1, spans)
    def _(i):
        tok_copy(1, i).start()

    order = jnp.concatenate([order_ref[0:1, c * tok : (c + 1) * tok] for c in range(spans)], axis=0)
    arriving = lax.shift_right_logical(order, bits) == s
    arrive = jnp.where(arriving, 1.0, 0.0)
    rank_in = dot(arrive.astype(BF16), before)
    rank_ref[...] = jnp.where(arriving, rank_in, -1.0)
    local = lax.rem(order, tok)
    col = lax.rem(local, cols)
    quadrant = (local // cols) * 2 + lax.rem(col, 2)
    code_ref[...] = jnp.where(arriving, quadrant * mt + col // 2 + 1, 0).astype(F32)

    @pl.loop(0, spans)
    def _(c):
        rk = rank_ref[pl.ds(c, 1), :]
        cd = code_ref[pl.ds(c, 1), :]
        row = lax.broadcasted_iota(jnp.int32, (slot, tok), 0)
        k = jnp.where(row >= cap, row - cap, row).astype(F32)
        to = jnp.sum(jnp.where(rk == k, cd, 0.0), axis=1, keepdims=True).astype(jnp.int32)
        row = lax.broadcasted_iota(jnp.int32, (slot, 2 * tok), 0)
        lane = lax.broadcasted_iota(jnp.int32, (slot, 2 * tok), 1)
        wanted = jnp.where(row >= cap, lane - tok, lane) + 1
        wanted = jnp.where(wanted > tok, 0, wanted)
        place_ref[pl.ds(pl.multiple_of(c * slot, slot), slot), :] = one_hot(
            jnp.logical_and(to == wanted, wanted > 0)
        )

    def ring_step(k):
        ring_copy(0, k).wait_recv()
        ring_copy(1, k).wait_recv()
        if k < steps:
            ring_copy(0, k + 1).start()
            ring_copy(1, k + 1).start()
        share_copy(k).start()
        if k < steps:
            share_copy(nz - k).start()

    ring_step(1)
    w_copy.wait()

    @pl.loop(0, 8)
    def _(t):
        q, h = t // 2, lax.rem(t, 2)
        w_rows = w_ref[pl.ds(pl.multiple_of(t * half, half), half), :]
        g = dot(cot_ref[0], w_rows, NT).astype(BF16)
        grad_ref[pl.ds(pl.multiple_of(h * tok + q * mt, mt), mt), :] = g

    ring_step(2)

    @pl.loop(0, 4)
    def _(t):
        place = place_ref[pl.ds(pl.multiple_of(t * rows, rows), rows), :]
        back = dot(place, grad_ref[...]).astype(BF16)
        back_ref[pl.ds(t * group, group)] = back.reshape(group, slot, half)

    ret_ref[s] = back_ref[s]
    ring_step(3)

    def settle(h):
        @pl.loop(1, spans)
        def _(i):
            tok_copy(h, i).wait_recv()

        arrived = recv_ref[h].reshape(spans * slot, quarter)
        for t in range(4):
            block = dot(place_ref[:, t * 2 * mt : (t + 1) * 2 * mt], arrived, TN).astype(BF16)
            part, q = t // 2, 2 * (t % 2)
            c = q * dm + h * half + part * quarter
            merged_ref[:, c : c + quarter] = block[:mt]
            merged_ref[:, c + dm : c + dm + quarter] = block[mt:]

        @pl.loop(0, views // 2)
        def _(t):
            per = groups // 2
            d = (t // per) * groups + h * per + lax.rem(t, per)

            @pl.when(d != v)
            def _():
                blk_copy(d).start()

    settle(0)
    settle(1)
    blocks_ref[v] = merged_ref[:, pl.ds(pl.multiple_of(v * width, width), width)]

    @pl.loop(1, spans)
    def _(i):
        back_copy(i).start()

    @pl.loop(0, 4)
    def _(t):
        at = pl.ds(pl.multiple_of(t * 256, 256), 256)
        o = dot(merged_ref[...], w_ref[:, at]) + bias_ref[0:1, at].astype(F32)
        merged_out_ref[0, :, at] = o.astype(BF16)

    ring_step(4)

    @pl.loop(0, nz)
    def _(k):
        share_copy(k).wait_recv()

    depth = views * mt
    lanes = 128
    sums = dot(jnp.ones((8, depth), BF16), cot_all[...].reshape(depth, dm))
    for i in range(dm // lanes):
        span_bias[s, i : i + 1, :] = sums[0:1, i * lanes : (i + 1) * lanes]

    @pl.loop(1, spans)
    def _(i):
        bias_copy(i).start()

    @pl.loop(1, views)
    def _(i):
        blk_copy(v ^ i).wait_recv()

    lhs = blocks_ref[...].reshape(depth, width)
    prod_a[...] = dot(lhs, cot_all[:, :, :, :half].reshape(depth, half), TN).reshape(prod_a.shape)

    @pl.loop(1, side)
    def _(i):
        sum_y(i).start()

    prod_b[...] = dot(lhs, cot_all[:, :, :, half:].reshape(depth, half), TN).reshape(prod_b.shape)

    @pl.loop(1, side)
    def _(i):
        sum_x(i).start()

    in_a[y] = prod_a[:, y]
    in_b[x] = prod_b[x]

    @pl.loop(1, side)
    def _(i):
        sum_y(i).wait_recv()

    part_a[...] = jnp.sum(in_a[...], axis=0)
    last_a[x] = part_a[x]

    @pl.loop(1, side)
    def _(i):
        last_x(i).start()

    @pl.loop(1, side)
    def _(i):
        sum_x(i).wait_recv()

    part_b[...] = jnp.sum(in_b[...], axis=0)
    last_b[y] = part_b[y]

    @pl.loop(1, side)
    def _(i):
        last_y(i).start()

    @pl.loop(1, spans)
    def _(i):
        back_copy(i).wait_recv()

    returned = ret_ref[...].reshape(spans * slot, half)
    for t in range(2):
        g = dot(pick_ref[:, t * tok : (t + 1) * tok], returned, TN)
        token_grad_ref[0, :, t * half : (t + 1) * half] = g.astype(BF16)

    @pl.loop(1, spans)
    def _(i):
        bias_copy(i).wait_recv()

    bias_grad_ref[...] = jnp.sum(span_bias[...], axis=0) * scale

    @pl.loop(1, side)
    def _(i):
        last_x(i).wait_recv()
        last_y(i).wait_recv()

    weight_grad_ref[:, :half] = jnp.sum(last_a[...], axis=0) * scale
    weight_grad_ref[:, half:] = jnp.sum(last_b[...], axis=0) * scale

    @pl.loop(1, spans)
    def _(i):
        tok_copy(0, i).wait_send()
        tok_copy(1, i).wait_send()
        back_copy(i).wait_send()
        bias_copy(i).wait_send()

    @pl.loop(1, views)
    def _(i):
        blk_copy(v ^ i).wait_send()

    for k in range(1, steps + 1):
        ring_copy(0, k).wait_send()
        ring_copy(1, k).wait_send()

    @pl.loop(0, nz)
    def _(k):
        share_copy(k).wait_send()

    @pl.loop(1, side)
    def _(i):
        sum_y(i).wait_send()
        sum_x(i).wait_send()
        last_x(i).wait_send()
        last_y(i).wait_send()


def body(views, spans, tokens, scan_order, w_merge, bias, cotangent):
    tok, dm = tokens.shape[1:]
    merge_in, do = w_merge.shape
    mt = tok // 4
    half, quarter = dm // 2, dm // 4
    slot = 3 * (tok // spans)
    width = merge_in // views
    part = merge_in // (views * spans)
    side = 4
    nz = views // 2
    scale = 1.0 / math.sqrt(views * spans * mt)
    vmem = pl.BlockSpec(memory_space=pltpu.VMEM)
    dma = pltpu.SemaphoreType.DMA
    merged_out, token_grad, weight_grad, bias_grad = pl.pallas_call(
        functools.partial(kernel, views, spans, 128, scale),
        out_shape=(
            jax.ShapeDtypeStruct((1, mt, do), BF16),
            jax.ShapeDtypeStruct((1, tok, dm), BF16),
            jax.ShapeDtypeStruct((part, do), F32),
            jax.ShapeDtypeStruct((do // 128, 128), F32),
        ),
        in_specs=[vmem, vmem, pl.BlockSpec(memory_space=pl.ANY), vmem, vmem],
        out_specs=(vmem, vmem, vmem, vmem),
        scratch_shapes=[
            pltpu.VMEM((merge_in, do), BF16),
            pltpu.VMEM((2, spans, slot, quarter), BF16),
            pltpu.VMEM((2, spans, slot, quarter), BF16),
            pltpu.VMEM((spans, slot, half), BF16),
            pltpu.VMEM((spans, slot, half), BF16),
            pltpu.VMEM((spans * slot, 2 * tok), BF16),
            pltpu.VMEM((spans * slot, 2 * tok), BF16),
            pltpu.VMEM((spans, tok), F32),
            pltpu.VMEM((spans, tok), F32),
            pltpu.VMEM((mt, merge_in), BF16),
            pltpu.VMEM((2 * tok, half), BF16),
            pltpu.VMEM((views, mt, width), BF16),
            pltpu.VMEM((nz, 2, mt, do), BF16),
            pltpu.VMEM((side, side, part, half), F32),
            pltpu.VMEM((side, side, part, half), F32),
            pltpu.VMEM((side, side, part, half), F32),
            pltpu.VMEM((side, side, part, half), F32),
            pltpu.VMEM((side, part, half), F32),
            pltpu.VMEM((side, part, half), F32),
            pltpu.VMEM((side, part, half), F32),
            pltpu.VMEM((side, part, half), F32),
            pltpu.VMEM((spans, do // 128, 128), F32),
            dma,
            dma((2 * spans,)),
            dma((2 * spans,)),
            dma((spans,)),
            dma((spans,)),
            dma((views,)),
            dma((views,)),
            dma((nz + 2,)),
            dma((nz + 2,)),
            dma((nz,)),
            dma((nz,)),
            dma((spans,)),
            dma((spans,)),
            dma((2 * side,)),
            dma((2 * side,)),
            dma((2 * side,)),
            dma((2 * side,)),
        ],
        compiler_params=pltpu.CompilerParams(
            collective_id=0, has_side_effects=True, vmem_limit_bytes=48 * 2**20
        ),
    )(tokens, scan_order, w_merge, bias.reshape(1, do), cotangent)
    return merged_out, token_grad, weight_grad, bias_grad.reshape(do)


def solution(mesh):
    in_specs = (P("view", "span", None), P("view", None), P(), P(), P("view", "span", None))
    out_specs = (P("view", "span", None), P("view", "span", None), P(("view", "span"), None), P())
    return jax.shard_map(
        functools.partial(body, mesh.shape["view"], mesh.shape["span"]),
        mesh=mesh,
        in_specs=in_specs,
        out_specs=out_specs,
        check_vma=False,
    )
```

time: 107 us -> 60 us (0.56)
  the two profiles are of different devices: /device:TPU:1 before, /device:TPU:32 now
where the time goes in v2:
time: 60 us; the launch traced here: 59.8 us
  Pallas kernels  53.1 us (88%)
  local copies, waits for them, and re-layouts  6.02 us (10%)
  between operations  0.64 us (1%)
    pallas_call x1, Pallas kernels, body(): pl.pallas_call(functools.partial(kernel, views, spans, 128, scale), out_s...  53.1 us
    unnamed x10, local copies, waits for them, and re-layouts  5.33 us

profile of v2, /device:TPU:32, one launch (start us, length us, event | category | flops | bytes accessed | tf_op | source)
XLA Modules:
  0.0 59.8 jit_solution(7780477711019328986)
XLA Ops:
  0.6 0.7 %reshape.14.bias_ref = bf16[1,1024]{1,0:T(2,128)(2,1)S(1)} reshape(bf16[1024]{0:T(1024)(128)(2,1)} %param.8) | data formatting | bytes 4096 | tf_op jit(solution)/shard_map/reshape | solution.py:493
  1.3 0.0 copy-start
  1.3 1.0 %copy-done = bf16[1,256,1024]{2,1,0:T(8,128)(2,1)S(1)} copy-done((bf16[1,256,1024]{2,1,0:T(8,128)(2,1)S(1)}, bf16[1,256,1024]{2,1,0:T(8,128)(2,1)}, u32[]{:S(2)}) %copy-start) | copy-done | bytes 524312
  2.4 0.0 copy-start.1
  2.4 0.9 %copy-done.1 = bf16[1,64,1024]{2,1,0:T(8,128)(2,1)S(1)} copy-done((bf16[1,64,1024]{2,1,0:T(8,128)(2,1)S(1)}, bf16[1,64,1024]{2,1,0:T(8,128)(2,1)}, u32[]{:S(2)}) %copy-start.1) | copy-done | bytes 131096
  3.3 0.0 copy-start.2
  3.3 0.7 %copy-done.2 = s32[1,4096]{1,0:T(1,128)S(1)} copy-done((s32[1,4096]{1,0:T(1,128)S(1)}, s32[1,4096]{1,0:T(1,128)}, u32[]{:S(2)}) %copy-start.2) | copy-done | bytes 16408
  4.0 53.1 %shard_map.84 = (bf16[1,64,1024]{2,1,0:T(8,128)(2,1)S(1)}, bf16[1,256,1024]{2,1,0:T(8,128)(2,1)S(1)}, f32[16,1024]{1,0:T(8,128)S(1)}, f32[8,128]{1,0:T(8,128)S(1)}) custom-call(bf16[1,256,1024]{2,1,0:T(8,128)(2,1)S(1)} %copy-done, s32[1,4096]{1,0:T(1,128)S(1)} %copy-done.2, bf16[4096,1024]{1,0:T(8,128)(2,1)} %w_hbm.1, bf16[1,1024]{1,0:T(2,128)(2,1)S(1)} %reshape.14.bias_ref, ...), custom_call_target="tpu_custom_call" | custom-call | tf_op jit(solution)/shard_map/pallas_call | solution.py:439
  57.1 0.7 %copy.13 = bf16[1,64,1024]{2,1,0:T(8,128)(2,1)} copy(bf16[1,64,1024]{2,1,0:T(8,128)(2,1)S(1)} %get-tuple-element.16) | data formatting | bytes 262144
  57.8 0.8 %copy.14 = bf16[1,256,1024]{2,1,0:T(8,128)(2,1)} copy(bf16[1,256,1024]{2,1,0:T(8,128)(2,1)S(1)} %get-tuple-element.17) | data formatting | bytes 1048576
  58.6 0.6 %copy.15 = f32[16,1024]{1,0:T(8,128)} copy(f32[16,1024]{1,0:T(8,128)S(1)} %get-tuple-element.18) | data formatting | bytes 131072
  59.2 0.6 copy.16
Async XLA Ops:
  1.3 1.0 %copy-start = (bf16[1,256,1024]{2,1,0:T(8,128)(2,1)S(1)}, bf16[1,256,1024]{2,1,0:T(8,128)(2,1)}, u32[]{:S(2)}) copy-start(bf16[1,256,1024]{2,1,0:T(8,128)(2,1)} %tokens_ref.1) | copy-start | bytes 1572868
  2.4 0.9 %copy-start.1 = (bf16[1,64,1024]{2,1,0:T(8,128)(2,1)S(1)}, bf16[1,64,1024]{2,1,0:T(8,128)(2,1)}, u32[]{:S(2)}) copy-start(bf16[1,64,1024]{2,1,0:T(8,128)(2,1)} %cot_ref.1) | copy-start | bytes 393220
  3.3 0.7 %copy-start.2 = (s32[1,4096]{1,0:T(1,128)S(1)}, s32[1,4096]{1,0:T(1,128)}, u32[]{:S(2)}) copy-start(s32[1,4096]{1,0:T(1,128)} %order_ref.1) | copy-start | bytes 49156

commit v3 on v2

v3 whole, which is shorter than its diff:
```python
import functools
import math

import jax
import jax.numpy as jnp
from jax import lax
from jax.experimental import pallas as pl
from jax.experimental.pallas import tpu as pltpu
from jax.sharding import PartitionSpec as P

MESH = pl.DeviceIdType.MESH
F32 = jnp.float32
BF16 = jnp.bfloat16
NN = (((1,), (0,)), ((), ()))
NT = (((1,), (1,)), ((), ()))
TN = (((0,), (0,)), ((), ()))


def dot(a, b, dims=NN):
    return lax.dot_general(a, b, dims, preferred_element_type=F32)


def one_hot(hit):
    return jnp.where(hit, 1.0, 0.0).astype(BF16)


def kernel(
    views,
    spans,
    cols,
    scale,
    tokens_hbm,
    order_hbm,
    w_hbm,
    bias_ref,
    cot_hbm,
    merged_out_ref,
    token_grad_ref,
    weight_grad_ref,
    bias_grad_ref,
    w_ref,
    tokens_ref,
    order_ref,
    out_ref,
    recv_ref,
    back_ref,
    ret_ref,
    pick_ref,
    place_ref,
    rank_ref,
    code_ref,
    merged_ref,
    grad_ref,
    blocks_ref,
    cot_all,
    prod_a,
    prod_b,
    in_a,
    in_b,
    part_a,
    part_b,
    last_a,
    last_b,
    span_bias,
    in_sem,
    tok_send,
    tok_recv,
    back_send,
    back_recv,
    blk_send,
    blk_recv,
    ring_send,
    ring_recv,
    share_send,
    share_recv,
    bias_send,
    bias_recv,
    sum_a_send,
    sum_a_recv,
    sum_b_send,
    sum_b_recv,
    last_a_send,
    last_a_recv,
    last_b_send,
    last_b_recv,
):
    v = lax.axis_index("view")
    s = lax.axis_index("span")
    core = lax.rem(v, 2)
    z = v // 2
    nz = views // 2
    steps = nz // 2
    side = 4
    x, y = s // side, lax.rem(s, side)
    mine_half = x // 2
    tok, dm = tokens_ref.shape
    half = dm // 2
    mt = tok // 4
    cap = 3 * (tok // spans) // 2
    slot = 2 * cap
    lanes = blocks_ref.shape[3]
    width = 2 * lanes
    na = prod_a.shape[4]

    order_in = pltpu.make_async_copy(order_hbm, order_ref, in_sem.at[0])
    tokens_in = pltpu.make_async_copy(tokens_hbm.at[0], tokens_ref, in_sem.at[1])
    cot_in = pltpu.make_async_copy(cot_hbm.at[0], cot_all.at[z, core], in_sem.at[2])
    w_in = pltpu.make_async_copy(w_hbm, w_ref, in_sem.at[3])
    order_in.start()
    tokens_in.start()
    cot_in.start()

    barrier = pltpu.get_barrier_semaphore()

    @pl.loop(1, spans)
    def _(i):
        pl.semaphore_signal(barrier, inc=1, device_id=(v, s ^ i), device_id_type=MESH)

    @pl.loop(1, views)
    def _(i):
        pl.semaphore_signal(barrier, inc=1, device_id=(v ^ i, s), device_id_type=MESH)

    w_in.start()

    def remote(src, dst, send, recv, device):
        return pltpu.make_async_remote_copy(
            src_ref=src,
            dst_ref=dst,
            send_sem=send,
            recv_sem=recv,
            device_id=device,
            device_id_type=MESH,
        )

    def tok_copy(h, i):
        at = h * spans + i
        return remote(
            out_ref.at[h, s ^ i], recv_ref.at[h, s], tok_send.at[at], tok_recv.at[at], (v, s ^ i)
        )

    def back_copy(i):
        return remote(
            back_ref.at[s ^ i], ret_ref.at[s], back_send.at[i], back_recv.at[i], (v, s ^ i)
        )

    def blk_copy(h, i):
        d = v ^ i
        at = h * views + i
        src = merged_ref.at[:, pl.ds(pl.multiple_of(d * width + h * lanes, lanes), lanes)]
        return remote(src, blocks_ref.at[h, v], blk_send.at[at], blk_recv.at[at], (d, s))

    def near(k):
        return lax.rem(z + 2 * nz - k, nz)

    def ring_copy(way, k):
        held = near(k - 1) if way == 0 else near(1 - k)
        to = near(-1) if way == 0 else near(1)
        ref = cot_all.at[held, core]
        if k == steps:
            ref = ref.at[:, way * half : (way + 1) * half]
        at = way * (steps + 1) + k
        return remote(ref, ref, ring_send.at[at], ring_recv.at[at], (to * 2 + core, s))

    def share_copy(k):
        ref = cot_all.at[near(k), core]
        return remote(ref, ref, share_send.at[k], share_recv.at[k], (v ^ 1, s))

    def bias_copy(i):
        ref = span_bias.at[s]
        return remote(ref, ref, bias_send.at[i], bias_recv.at[i], (v, s ^ i))

    def sum_a(h, i):
        at = h * side + i
        return remote(
            prod_a.at[h, :, y ^ i], in_a.at[h, y], sum_a_send.at[at], sum_a_recv.at[at], (v, s ^ i)
        )

    def sum_b(h, t, k):
        to = (2 * h + t) * side + y
        return remote(
            prod_b.at[h, t], in_b.at[k], sum_b_send.at[2 * h + t], sum_b_recv.at[k], (v, to)
        )

    def last_a_copy(h, t, k):
        to = (2 * h + t) * side + y
        return remote(
            part_a.at[h, t], last_a.at[k], last_a_send.at[2 * h + t], last_a_recv.at[k], (v, to)
        )

    def last_b_copy(i):
        return remote(
            part_b.at[y ^ i], last_b.at[y], last_b_send.at[i], last_b_recv.at[i], (v, s ^ i)
        )

    def pair_up(rows):
        n = rows.shape[1] // 2
        a = rows[:, :n].reshape(spans, cap, n)
        b = rows[:, n:].reshape(spans, cap, n)
        return jnp.concatenate([a, b], axis=1).astype(BF16)

    def unpair(slots):
        wide = slots.astype(F32)
        n = wide.shape[2]
        a = wide[:, :cap].reshape(spans * cap, n)
        b = wide[:, cap:].reshape(spans * cap, n)
        return jnp.concatenate([a, b], axis=1).astype(BF16)

    before = one_hot(
        lax.broadcasted_iota(jnp.int32, (tok, tok), 0)
        < lax.broadcasted_iota(jnp.int32, (tok, tok), 1)
    )
    bits = int(math.log2(tok))
    order_in.wait()
    mine = order_ref[0:1, pl.ds(pl.multiple_of(s * tok, tok), tok)]
    owner = lax.shift_right_logical(mine, bits)
    hot = jnp.where(lax.broadcasted_iota(jnp.int32, (spans, tok), 0) == owner, 1.0, 0.0)
    rank = jnp.sum(dot(hot.astype(BF16), before) * hot, axis=0, keepdims=True).astype(jnp.int32)
    to_slot = owner * cap + rank
    pick_ref[...] = one_hot(lax.broadcasted_iota(jnp.int32, (spans * cap, tok), 0) == to_slot)
    tokens_in.wait()

    def pieces(h):
        return [c + h * lanes for c in range(0, dm, width)]

    def fill(h):
        part = jnp.concatenate([tokens_ref[:, c : c + lanes] for c in pieces(h)], axis=1)
        out_ref[h] = pair_up(dot(pick_ref[...], part))
        recv_ref[h, s] = out_ref[h, s]

    fill(0)
    cot_in.wait()
    pl.semaphore_wait(barrier, spans + views - 2)
    ring_copy(0, 1).start()
    ring_copy(1, 1).start()

    @pl.loop(1, spans)
    def _(i):
        tok_copy(0, i).start()

    share_copy(0).start()
    fill(1)

    @pl.loop(1, spans)
    def _(i):
        tok_copy(1, i).start()

    order = jnp.concatenate([order_ref[0:1, c * tok : (c + 1) * tok] for c in range(spans)], axis=0)
    arriving = lax.shift_right_logical(order, bits) == s
    arrive = jnp.where(arriving, 1.0, 0.0)
    rank_in = dot(arrive.astype(BF16), before)
    rank_ref[...] = jnp.where(arriving, rank_in, -1.0)
    local = lax.rem(order, tok)
    col = lax.rem(local, cols)
    quadrant = (local // cols) * 2 + lax.rem(col, 2)
    code_ref[...] = jnp.where(arriving, quadrant * mt + col // 2 + 1, 0).astype(F32)

    @pl.loop(0, spans // 2)
    def _(t):
        k = lax.broadcasted_iota(jnp.int32, (cap, tok), 0).astype(F32)
        lane = lax.broadcasted_iota(jnp.int32, (cap, tok), 1).astype(F32) + 1.0
        found = []
        for c in range(2):
            rk = rank_ref[pl.ds(2 * t + c, 1), :]
            cd = code_ref[pl.ds(2 * t + c, 1), :]
            to = jnp.sum(jnp.where(rk == k, cd, 0.0), axis=1, keepdims=True)
            found.append(jnp.where(to == lane, 1.0, 0.0))
        place_ref[pl.ds(pl.multiple_of(t * slot, slot), slot), :] = jnp.concatenate(
            found, axis=0
        ).astype(BF16)

    def ring_step(k):
        ring_copy(0, k).wait_recv()
        ring_copy(1, k).wait_recv()
        if k < steps:
            ring_copy(0, k + 1).start()
            ring_copy(1, k + 1).start()
        share_copy(k).start()
        if k < steps:
            share_copy(nz - k).start()

    ring_step(1)
    w_in.wait()

    @pl.loop(0, 4)
    def _(q):
        w_rows = w_ref[pl.ds(pl.multiple_of(q * dm, dm), dm), :]
        g = dot(cot_all[z, core], w_rows, NT).astype(BF16)
        grad_ref[pl.ds(pl.multiple_of(q * mt, mt), mt), :] = g

    ring_step(2)

    def settle(h):
        @pl.loop(1, spans)
        def _(i):
            tok_copy(h, i).wait_recv()

        block = dot(place_ref[...], unpair(recv_ref[h]), TN).astype(BF16)
        for q in range(4):
            for n, c in enumerate(pieces(h)):
                merged_ref[:, q * dm + c : q * dm + c + lanes] = block[
                    q * mt : (q + 1) * mt, n * lanes : (n + 1) * lanes
                ]
        at = pl.ds(pl.multiple_of(v * width + h * lanes, lanes), lanes)
        blocks_ref[h, v] = merged_ref[:, at]

        @pl.loop(1, views)
        def _(i):
            blk_copy(h, i).start()

    settle(0)
    ring_step(3)
    back_ref[...] = pair_up(dot(place_ref[...], grad_ref[...]))
    ret_ref[s] = back_ref[s]
    settle(1)

    @pl.loop(1, spans)
    def _(i):
        back_copy(i).start()

    @pl.loop(0, 4)
    def _(t):
        at = pl.ds(pl.multiple_of(t * 256, 256), 256)
        o = dot(merged_ref[...], w_ref[:, at]) + bias_ref[0:1, at].astype(F32)
        merged_out_ref[0, :, at] = o.astype(BF16)

    ring_step(4)

    @pl.loop(0, nz)
    def _(k):
        share_copy(k).wait_recv()

    depth = views * mt

    def multiply(h):
        @pl.loop(1, views)
        def _(i):
            blk_copy(h, i).wait_recv()

        lhs = blocks_ref[h].reshape(depth, lanes)
        prod_a[h] = dot(lhs, cot_all[:, :, :, :na].reshape(depth, na), TN).reshape(
            prod_a.shape[1:]
        )

        @pl.loop(1, side)
        def _(i):
            sum_a(h, i).start()

        prod_b[h] = dot(lhs, cot_all[:, :, :, na:].reshape(depth, dm - na), TN).reshape(
            prod_b.shape[1:]
        )
        for t in range(2):

            @pl.when(x != 2 * h + t)
            def _():
                sum_b(h, t, x).start()

            @pl.when(x == 2 * h + t)
            def _():
                in_b[x] = prod_b[h, t]

        in_a[h, y] = prod_a[h, :, y]

    def combine(h):
        @pl.loop(1, side)
        def _(i):
            sum_a(h, i).wait_recv()

        part_a[h] = jnp.sum(in_a[h], axis=0)
        for t in range(2):

            @pl.when(x != 2 * h + t)
            def _():
                last_a_copy(h, t, x).start()

            @pl.when(x == 2 * h + t)
            def _():
                last_a[x] = part_a[h, t]

        @pl.when(mine_half == h)
        def _():
            @pl.loop(1, side)
            def _(i):
                sum_b(h, 0, x ^ i).wait_recv()

            part_b[...] = jnp.sum(in_b[...], axis=0)
            last_b[y] = part_b[y]

            @pl.loop(1, side)
            def _(i):
                last_b_copy(i).start()

    multiply(0)

    sums = dot(jnp.ones((8, depth), BF16), cot_all[...].reshape(depth, dm))
    for i in range(dm // 128):
        span_bias[s, i : i + 1, :] = sums[0:1, i * 128 : (i + 1) * 128]

    @pl.loop(1, spans)
    def _(i):
        bias_copy(i).start()

    multiply(1)
    combine(0)
    combine(1)

    @pl.loop(1, spans)
    def _(i):
        back_copy(i).wait_recv()

    token_grad_ref[0] = dot(pick_ref[...], unpair(ret_ref[...]), TN).astype(BF16)

    @pl.loop(1, spans)
    def _(i):
        bias_copy(i).wait_recv()

    bias_grad_ref[...] = jnp.sum(span_bias[...], axis=0) * scale

    @pl.loop(1, side)
    def _(i):
        last_a_copy(0, 0, x ^ i).wait_recv()
        last_b_copy(i).wait_recv()

    weight_grad_ref[:, :na] = jnp.sum(last_a[...], axis=0) * scale
    weight_grad_ref[:, na:] = jnp.sum(last_b[...], axis=0) * scale

    @pl.loop(1, spans)
    def _(i):
        tok_copy(0, i).wait_send()
        tok_copy(1, i).wait_send()
        back_copy(i).wait_send()
        bias_copy(i).wait_send()

    @pl.loop(1, views)
    def _(i):
        blk_copy(0, i).wait_send()
        blk_copy(1, i).wait_send()

    for k in range(1, steps + 1):
        ring_copy(0, k).wait_send()
        ring_copy(1, k).wait_send()

    @pl.loop(0, nz)
    def _(k):
        share_copy(k).wait_send()

    @pl.loop(1, side)
    def _(i):
        sum_a(0, i).wait_send()
        sum_a(1, i).wait_send()
        last_b_copy(i).wait_send()

    for h in range(2):
        for t in range(2):

            @pl.when(x != 2 * h + t)
            def _():
                sum_b(h, t, x).wait_send()
                last_a_copy(h, t, x).wait_send()


def body(views, spans, tokens, scan_order, w_merge, bias, cotangent):
    tok, dm = tokens.shape[1:]
    merge_in, do = w_merge.shape
    mt = tok // 4
    half = dm // 2
    cap = 3 * (tok // spans) // 2
    slot = 2 * cap
    lanes = merge_in // views // 2
    part = merge_in // (views * spans)
    side = 4
    nz = views // 2
    na = 5 * do // 8
    nb = do - na
    scale = 1.0 / math.sqrt(views * spans * mt)
    vmem = pl.BlockSpec(memory_space=pltpu.VMEM)
    hbm = pl.BlockSpec(memory_space=pl.ANY)
    dma = pltpu.SemaphoreType.DMA
    merged_out, token_grad, weight_grad, bias_grad = pl.pallas_call(
        functools.partial(kernel, views, spans, 128, scale),
        out_shape=(
            jax.ShapeDtypeStruct((1, mt, do), BF16),
            jax.ShapeDtypeStruct((1, tok, dm), BF16),
            jax.ShapeDtypeStruct((part, do), F32),
            jax.ShapeDtypeStruct((do // 128, 128), F32),
        ),
        in_specs=[hbm, hbm, hbm, vmem, hbm],
        out_specs=(vmem, vmem, vmem, vmem),
        scratch_shapes=[
            pltpu.VMEM((merge_in, do), BF16),
            pltpu.VMEM((tok, dm), BF16),
            pltpu.VMEM((1, spans * tok), jnp.int32),
            pltpu.VMEM((2, spans, slot, half // 2), BF16),
            pltpu.VMEM((2, spans, slot, half // 2), BF16),
            pltpu.VMEM((spans, slot, half), BF16),
            pltpu.VMEM((spans, slot, half), BF16),
            pltpu.VMEM((spans * cap, tok), BF16),
            pltpu.VMEM((spans * cap, tok), BF16),
            pltpu.VMEM((spans, tok), F32),
            pltpu.VMEM((spans, tok), F32),
            pltpu.VMEM((mt, merge_in), BF16),
            pltpu.VMEM((tok, dm), BF16),
            pltpu.VMEM((2, views, mt, lanes), BF16),
            pltpu.VMEM((nz, 2, mt, do), BF16),
            pltpu.VMEM((2, 2, side, part, na), F32),
            pltpu.VMEM((2, 2, side, part, nb), F32),
            pltpu.VMEM((2, side, 2, part, na), F32),
            pltpu.VMEM((side, side, part, nb), F32),
            pltpu.VMEM((2, 2, part, na), F32),
            pltpu.VMEM((side, part, nb), F32),
            pltpu.VMEM((side, part, na), F32),
            pltpu.VMEM((side, part, nb), F32),
            pltpu.VMEM((spans, do // 128, 128), F32),
            dma((4,)),
            dma((2 * spans,)),
            dma((2 * spans,)),
            dma((spans,)),
            dma((spans,)),
            dma((2 * views,)),
            dma((2 * views,)),
            dma((nz + 2,)),
            dma((nz + 2,)),
            dma((nz,)),
            dma((nz,)),
            dma((spans,)),
            dma((spans,)),
            dma((2 * side,)),
            dma((2 * side,)),
            dma((side,)),
            dma((side,)),
            dma((side,)),
            dma((side,)),
            dma((side,)),
            dma((side,)),
        ],
        compiler_params=pltpu.CompilerParams(
            collective_id=0, has_side_effects=True, vmem_limit_bytes=60 * 2**20
        ),
    )(tokens, scan_order, w_merge, bias.reshape(1, do), cotangent)
    return merged_out, token_grad, weight_grad, bias_grad.reshape(do)


def solution(mesh):
    in_specs = (P("view", "span", None), P("view", None), P(), P(), P("view", "span", None))
    out_specs = (P("view", "span", None), P("view", "span", None), P(("view", "span"), None), P())
    return jax.shard_map(
        functools.partial(body, mesh.shape["view"], mesh.shape["span"]),
        mesh=mesh,
        in_specs=in_specs,
        out_specs=out_specs,
        check_vma=False,
    )
```

time: 60 us -> 60.7 us (1.012)
  the two profiles are of different devices: /device:TPU:32 before, /device:TPU:23 now
where the time goes in v3:
time: 60.7 us; the launch traced here: 59.7 us
  Pallas kernels  51.6 us (85%)
  local copies, waits for them, and re-layouts  7.46 us (12%)
  between operations  0.64 us (1%)
    pallas_call x1, Pallas kernels, body(): pl.pallas_call(functools.partial(kernel, views, spans, 128, scale), out_s...  51.6 us
    unnamed x4, local copies, waits for them, and re-layouts  6.18 us
    reshape x1, local copies, waits for them, and re-layouts, body(): bias.reshape(1, do)  1.28 us

profile of v3, /device:TPU:23, one launch (start us, length us, event | category | flops | bytes accessed | tf_op | source)
XLA Modules:
  0.0 59.7 jit_solution(1389504564446922489)
XLA Ops:
  0.6 1.3 %reshape.14.bias_ref = bf16[1,1024]{1,0:T(2,128)(2,1)} reshape(bf16[1024]{0:T(1024)(128)(2,1)} %param.8) | data formatting | bytes 4096 | tf_op jit(solution)/shard_map/reshape | solution.py:538
  1.9 51.6 %shard_map.84 = (bf16[1,64,1024]{2,1,0:T(8,128)(2,1)}, bf16[1,256,1024]{2,1,0:T(8,128)(2,1)}, f32[16,1024]{1,0:T(8,128)}, f32[8,128]{1,0:T(8,128)}) custom-call(bf16[1,256,1024]{2,1,0:T(8,128)(2,1)} %tokens_hbm.1, s32[1,4096]{1,0:T(1,128)} %order_hbm.1, bf16[4096,1024]{1,0:T(8,128)(2,1)} %w_hbm.1, bf16[1,1024]{1,0:T(2,128)(2,1)} %reshape.14.bias_ref, ...), custom_call_target="tpu_custom_call" | custom-call | tf_op jit(solution)/shard_map/pallas_call | solution.py:478
  53.5 1.6 %copy.13 = bf16[1,64,1024]{2,1,0:T(8,128)(2,1)} copy(bf16[1,64,1024]{2,1,0:T(8,128)(2,1)} %get-tuple-element.16) | data formatting | bytes 262144
  55.1 1.9 %copy.14 = bf16[1,256,1024]{2,1,0:T(8,128)(2,1)} copy(bf16[1,256,1024]{2,1,0:T(8,128)(2,1)} %get-tuple-element.17) | data formatting | bytes 1048576
  56.9 1.5 %copy.15 = f32[16,1024]{1,0:T(8,128)} copy(f32[16,1024]{1,0:T(8,128)} %get-tuple-element.18) | data formatting | bytes 131072
  58.4 1.3 %copy.16 = f32[1024]{0:T(1024)} copy(f32[1024]{0:T(1024)} %bitcast.1) | data formatting | bytes 8192

commit v4 on v3

--- a/solution.py
+++ b/solution.py
@@ -32,8 +32,12 @@
     tokens_hbm,
     order_hbm,
     w_hbm,
-    bias_ref,
+    bias_hbm,
     cot_hbm,
+    merged_out_hbm,
+    token_grad_hbm,
+    weight_grad_hbm,
+    bias_grad_hbm,
     merged_out_ref,
     token_grad_ref,
     weight_grad_ref,
@@ -41,6 +45,7 @@
     w_ref,
     tokens_ref,
     order_ref,
+    bias_ref,
     out_ref,
     recv_ref,
     back_ref,
@@ -106,6 +111,11 @@
     tokens_in = pltpu.make_async_copy(tokens_hbm.at[0], tokens_ref, in_sem.at[1])
     cot_in = pltpu.make_async_copy(cot_hbm.at[0], cot_all.at[z, core], in_sem.at[2])
     w_in = pltpu.make_async_copy(w_hbm, w_ref, in_sem.at[3])
+    bias_in = pltpu.make_async_copy(bias_hbm, bias_ref, in_sem.at[4])
+    merged_put = pltpu.make_async_copy(merged_out_ref, merged_out_hbm, in_sem.at[5])
+    tokens_put = pltpu.make_async_copy(token_grad_ref, token_grad_hbm, in_sem.at[6])
+    weight_put = pltpu.make_async_copy(weight_grad_ref, weight_grad_hbm, in_sem.at[7])
+    bias_put = pltpu.make_async_copy(bias_grad_ref, bias_grad_hbm, in_sem.at[8])
     order_in.start()
     tokens_in.start()
     cot_in.start()
@@ -121,6 +131,7 @@
         pl.semaphore_signal(barrier, inc=1, device_id=(v ^ i, s), device_id_type=MESH)
 
     w_in.start()
+    bias_in.start()
 
     def remote(src, dst, send, recv, device):
         return pltpu.make_async_remote_copy(
@@ -287,6 +298,13 @@
         g = dot(cot_all[z, core], w_rows, NT).astype(BF16)
         grad_ref[pl.ds(pl.multiple_of(q * mt, mt), mt), :] = g
 
+    back_ref[...] = pair_up(dot(place_ref[...], grad_ref[...]))
+    ret_ref[s] = back_ref[s]
+
+    @pl.loop(1, spans)
+    def _(i):
+        back_copy(i).start()
+
     ring_step(2)
 
     def settle(h):
@@ -309,19 +327,17 @@
 
     settle(0)
     ring_step(3)
-    back_ref[...] = pair_up(dot(place_ref[...], grad_ref[...]))
-    ret_ref[s] = back_ref[s]
     settle(1)
 
-    @pl.loop(1, spans)
-    def _(i):
-        back_copy(i).start()
+    bias_in.wait()
 
     @pl.loop(0, 4)
     def _(t):
         at = pl.ds(pl.multiple_of(t * 256, 256), 256)
-        o = dot(merged_ref[...], w_ref[:, at]) + bias_ref[0:1, at].astype(F32)
+        o = dot(merged_ref[...], w_ref[:, at]) + bias_ref[at].astype(F32)[None, :]
         merged_out_ref[0, :, at] = o.astype(BF16)
+
+    merged_put.start()
 
     ring_step(4)
 
@@ -408,12 +424,14 @@
         back_copy(i).wait_recv()
 
     token_grad_ref[0] = dot(pick_ref[...], unpair(ret_ref[...]), TN).astype(BF16)
+    tokens_put.start()
 
     @pl.loop(1, spans)
     def _(i):
         bias_copy(i).wait_recv()
 
     bias_grad_ref[...] = jnp.sum(span_bias[...], axis=0) * scale
+    bias_put.start()
 
     @pl.loop(1, side)
     def _(i):
@@ -422,6 +440,7 @@
 
     weight_grad_ref[:, :na] = jnp.sum(last_a[...], axis=0) * scale
     weight_grad_ref[:, na:] = jnp.sum(last_b[...], axis=0) * scale
+    weight_put.start()
 
     @pl.loop(1, spans)
     def _(i):
@@ -456,6 +475,20 @@
             def _():
                 sum_b(h, t, x).wait_send()
                 last_a_copy(h, t, x).wait_send()
+
+    merged_put.wait()
+    tokens_put.wait()
+    bias_put.wait()
+    weight_put.wait()
+
+
+def hand_over(*refs):
+    n = (len(refs) - 1) // 2
+    copies = [pltpu.make_async_copy(refs[i], refs[n + i], refs[-1].at[i]) for i in range(n)]
+    for copy in copies:
+        copy.start()
+    for copy in copies:
+        copy.wait()
 
 
 def body(views, spans, tokens, scan_order, w_merge, bias, cotangent):
@@ -472,7 +505,6 @@
     na = 5 * do // 8
     nb = do - na
     scale = 1.0 / math.sqrt(views * spans * mt)
-    vmem = pl.BlockSpec(memory_space=pltpu.VMEM)
     hbm = pl.BlockSpec(memory_space=pl.ANY)
     dma = pltpu.SemaphoreType.DMA
     merged_out, token_grad, weight_grad, bias_grad = pl.pallas_call(
@@ -483,12 +515,17 @@
             jax.ShapeDtypeStruct((part, do), F32),
             jax.ShapeDtypeStruct((do // 128, 128), F32),
         ),
-        in_specs=[hbm, hbm, hbm, vmem, hbm],
-        out_specs=(vmem, vmem, vmem, vmem),
+        in_specs=[hbm] * 5,
+        out_specs=(hbm,) * 4,
         scratch_shapes=[
+            pltpu.VMEM((1, mt, do), BF16),
+            pltpu.VMEM((1, tok, dm), BF16),
+            pltpu.VMEM((part, do), F32),
+            pltpu.VMEM((do // 128, 128), F32),
             pltpu.VMEM((merge_in, do), BF16),
             pltpu.VMEM((tok, dm), BF16),
             pltpu.VMEM((1, spans * tok), jnp.int32),
+            pltpu.VMEM((do,), BF16),
             pltpu.VMEM((2, spans, slot, half // 2), BF16),
             pltpu.VMEM((2, spans, slot, half // 2), BF16),
             pltpu.VMEM((spans, slot, half), BF16),
@@ -510,7 +547,7 @@
             pltpu.VMEM((side, part, na), F32),
             pltpu.VMEM((side, part, nb), F32),
             pltpu.VMEM((spans, do // 128, 128), F32),
-            dma((4,)),
+            dma((9,)),
             dma((2 * spans,)),
             dma((2 * spans,)),
             dma((spans,)),
@@ -535,7 +572,15 @@
         compiler_params=pltpu.CompilerParams(
             collective_id=0, has_side_effects=True, vmem_limit_bytes=60 * 2**20
         ),
-    )(tokens, scan_order, w_merge, bias.reshape(1, do), cotangent)
+    )(tokens, scan_order, w_merge, bias, cotangent)
+    results = (merged_out, token_grad, weight_grad, bias_grad)
+    merged_out, token_grad, weight_grad, bias_grad = pl.pallas_call(
+        hand_over,
+        out_shape=tuple(jax.ShapeDtypeStruct(r.shape, r.dtype) for r in results),
+        in_specs=[hbm] * 4,
+        out_specs=(hbm,) * 4,
+        scratch_shapes=[dma((4,))],
+    )(*results)
     return merged_out, token_grad, weight_grad, bias_grad.reshape(do)
 
 

time: 60.7 us -> 74.5 us (1.23); the launches traced: 59.7 us -> 74.3 us
  Pallas kernels: 51.6 us -> 73.7 us
  local copies, waits for them, and re-layouts: 7.46 us -> 0 us
    pallas_call x0 -> x1, Pallas kernels: none -> 23.1 us  [body(): pl.pallas_call(hand_over, out_shape=tuple((jax.ShapeDtypeStruct(r.shape,...]
    unnamed x4 -> x0, local copies, waits for them, and re-layouts: 6.18 us -> none
    reshape x1 -> x0, local copies, waits for them, and re-layouts: 1.28 us -> none  [body(): bias.reshape(1, do)]
    pallas_call x1, Pallas kernels: 51.6 us -> 50.6 us  [body(): pl.pallas_call(functools.partial(kernel, views, spans, 128, scale), out_s...]
where the time goes in v4:
time: 74.5 us; the launch traced here: 74.3 us
  Pallas kernels  73.7 us (99%)
    pallas_call x1, Pallas kernels, body(): pl.pallas_call(functools.partial(kernel, views, spans, 128, scale), out_s...  50.6 us
    pallas_call x1, Pallas kernels, body(): pl.pallas_call(hand_over, out_shape=tuple((jax.ShapeDtypeStruct(r.shape,...  23.1 us

profile of v4, /device:TPU:23, one launch (start us, length us, event | category | flops | bytes accessed | tf_op | source)
XLA Modules:
  0.0 74.3 jit_solution(16426290362764794729)
XLA Ops:
  0.6 50.6 %shard_map.84 = (bf16[1,64,1024]{2,1,0:T(8,128)(2,1)}, bf16[1,256,1024]{2,1,0:T(8,128)(2,1)}, f32[16,1024]{1,0:T(8,128)}, f32[8,128]{1,0:T(8,128)}) custom-call(bf16[1,256,1024]{2,1,0:T(8,128)(2,1)} %tokens_hbm.1, s32[1,4096]{1,0:T(1,128)} %order_hbm.1, bf16[4096,1024]{1,0:T(8,128)(2,1)} %w_hbm.1, bf16[1024]{0:T(1024)(128)(2,1)} %bias_hbm.1, ...), custom_call_target="tpu_custom_call" | custom-call | tf_op jit(solution)/shard_map/pallas_call | solution.py:510
  51.2 23.1 %shard_map.85 = (bf16[1,64,1024]{2,1,0:T(8,128)(2,1)}, bf16[1,256,1024]{2,1,0:T(8,128)(2,1)}, f32[16,1024]{1,0:T(8,128)}, f32[8,128]{1,0:T(8,128)}) custom-call(bf16[1,64,1024]{2,1,0:T(8,128)(2,1)} %get-tuple-element.12.refs_0_, bf16[1,256,1024]{2,1,0:T(8,128)(2,1)} %get-tuple-element.13.refs_1_, f32[16,1024]{1,0:T(8,128)} %get-tuple-element.14.refs_2_, ...), custom_call_target="tpu_custom_call" | custom-call | tf_op jit(solution)/shard_map/pallas_call | solution.py:577

commit v5 on v4

--- a/solution.py
+++ b/solution.py
@@ -483,11 +483,16 @@
 
 
 def hand_over(*refs):
-    n = (len(refs) - 1) // 2
-    copies = [pltpu.make_async_copy(refs[i], refs[n + i], refs[-1].at[i]) for i in range(n)]
-    for copy in copies:
+    n = (len(refs) - 1) // 3
+    sems = refs[-1]
+    ins = [pltpu.make_async_copy(refs[i], refs[2 * n + i], sems.at[i]) for i in range(n)]
+    outs = [pltpu.make_async_copy(refs[2 * n + i], refs[n + i], sems.at[n + i]) for i in range(n)]
+    for copy in ins:
         copy.start()
-    for copy in copies:
+    for read, write in zip(ins, outs):
+        read.wait()
+        write.start()
+    for copy in outs:
         copy.wait()
 
 
@@ -579,7 +584,7 @@
         out_shape=tuple(jax.ShapeDtypeStruct(r.shape, r.dtype) for r in results),
         in_specs=[hbm] * 4,
         out_specs=(hbm,) * 4,
-        scratch_shapes=[dma((4,))],
+        scratch_shapes=[pltpu.VMEM(r.shape, r.dtype) for r in results] + [dma((8,))],
     )(*results)
     return merged_out, token_grad, weight_grad, bias_grad.reshape(do)
 

time: 74.5 us -> 53.4 us (0.72)
  Pallas kernels: 73.7 us -> 52.6 us
    pallas_call x1, Pallas kernels: 23.1 us -> 1.99 us  [body(): pl.pallas_call(hand_over, out_shape=tuple((jax.ShapeDtypeStruct(r.shape,...]
where the time goes in v5:
time: 53.4 us; the launch traced here: 53.2 us
  Pallas kernels  52.6 us (99%)
  between operations  0.64 us (1%)
    pallas_call x1, Pallas kernels, body(): pl.pallas_call(functools.partial(kernel, views, spans, 128, scale), out_s...  50.6 us
    pallas_call x1, Pallas kernels, body(): pl.pallas_call(hand_over, out_shape=tuple((jax.ShapeDtypeStruct(r.shape,...  1.99 us

profile of v5, /device:TPU:23, one launch (start us, length us, event | category | flops | bytes accessed | tf_op | source)
XLA Modules:
  0.0 53.2 jit_solution(10616007364987972769)
XLA Ops:
  0.6 50.6 %shard_map.84 = (bf16[1,64,1024]{2,1,0:T(8,128)(2,1)}, bf16[1,256,1024]{2,1,0:T(8,128)(2,1)}, f32[16,1024]{1,0:T(8,128)}, f32[8,128]{1,0:T(8,128)}) custom-call(bf16[1,256,1024]{2,1,0:T(8,128)(2,1)} %tokens_hbm.1, s32[1,4096]{1,0:T(1,128)} %order_hbm.1, bf16[4096,1024]{1,0:T(8,128)(2,1)} %w_hbm.1, bf16[1024]{0:T(1024)(128)(2,1)} %bias_hbm.1, ...), custom_call_target="tpu_custom_call" | custom-call | tf_op jit(solution)/shard_map/pallas_call | solution.py:515
  51.2 2.0 %shard_map.85 = (bf16[1,64,1024]{2,1,0:T(8,128)(2,1)}, bf16[1,256,1024]{2,1,0:T(8,128)(2,1)}, f32[16,1024]{1,0:T(8,128)}, f32[8,128]{1,0:T(8,128)}) custom-call(bf16[1,64,1024]{2,1,0:T(8,128)(2,1)} %get-tuple-element.12.refs_0_, bf16[1,256,1024]{2,1,0:T(8,128)(2,1)} %get-tuple-element.13.refs_1_, f32[16,1024]{1,0:T(8,128)} %get-tuple-element.14.refs_2_, ...), custom_call_target="tpu_custom_call" | custom-call | tf_op jit(solution)/shard_map/pallas_call | solution.py:582

commit v6 on v5

--- a/solution.py
+++ b/solution.py
@@ -329,6 +329,75 @@
     ring_step(3)
     settle(1)
 
+    ring_step(4)
+
+    @pl.loop(0, nz)
+    def _(k):
+        share_copy(k).wait_recv()
+
+    depth = views * mt
+
+    def multiply(h):
+        @pl.loop(1, views)
+        def _(i):
+            blk_copy(h, i).wait_recv()
+
+        lhs = blocks_ref[h].reshape(depth, lanes)
+        prod_a[h] = dot(lhs, cot_all[:, :, :, :na].reshape(depth, na), TN).reshape(
+            prod_a.shape[1:]
+        )
+
+        @pl.loop(1, side)
+        def _(i):
+            sum_a(h, i).start()
+
+        prod_b[h] = dot(lhs, cot_all[:, :, :, na:].reshape(depth, dm - na), TN).reshape(
+            prod_b.shape[1:]
+        )
+        for t in range(2):
+
+            @pl.when(x != 2 * h + t)
+            def _():
+                sum_b(h, t, x).start()
+
+            @pl.when(x == 2 * h + t)
+            def _():
+                in_b[x] = prod_b[h, t]
+
+        in_a[h, y] = prod_a[h, :, y]
+
+    def combine(h):
+        @pl.loop(1, side)
+        def _(i):
+            sum_a(h, i).wait_recv()
+
+        part_a[h] = jnp.sum(in_a[h], axis=0)
+        for t in range(2):
+
+            @pl.when(x != 2 * h + t)
+            def _():
+                last_a_copy(h, t, x).start()
+
+            @pl.when(x == 2 * h + t)
+            def _():
+                last_a[x] = part_a[h, t]
+
+        @pl.when(mine_half == h)
+        def _():
+            @pl.loop(1, side)
+            def _(i):
+                sum_b(h, 0, x ^ i).wait_recv()
+
+            part_b[...] = jnp.sum(in_b[...], axis=0)
+            last_b[y] = part_b[y]
+
+            @pl.loop(1, side)
+            def _(i):
+                last_b_copy(i).start()
+
+    multiply(0)
+    multiply(1)
+
     bias_in.wait()
 
     @pl.loop(0, 4)
@@ -339,74 +408,6 @@
 
     merged_put.start()
 
-    ring_step(4)
-
-    @pl.loop(0, nz)
-    def _(k):
-        share_copy(k).wait_recv()
-
-    depth = views * mt
-
-    def multiply(h):
-        @pl.loop(1, views)
-        def _(i):
-            blk_copy(h, i).wait_recv()
-
-        lhs = blocks_ref[h].reshape(depth, lanes)
-        prod_a[h] = dot(lhs, cot_all[:, :, :, :na].reshape(depth, na), TN).reshape(
-            prod_a.shape[1:]
-        )
-
-        @pl.loop(1, side)
-        def _(i):
-            sum_a(h, i).start()
-
-        prod_b[h] = dot(lhs, cot_all[:, :, :, na:].reshape(depth, dm - na), TN).reshape(
-            prod_b.shape[1:]
-        )
-        for t in range(2):
-
-            @pl.when(x != 2 * h + t)
-            def _():
-                sum_b(h, t, x).start()
-
-            @pl.when(x == 2 * h + t)
-            def _():
-                in_b[x] = prod_b[h, t]
-
-        in_a[h, y] = prod_a[h, :, y]
-
-    def combine(h):
-        @pl.loop(1, side)
-        def _(i):
-            sum_a(h, i).wait_recv()
-
-        part_a[h] = jnp.sum(in_a[h], axis=0)
-        for t in range(2):
-
-            @pl.when(x != 2 * h + t)
-            def _():
-                last_a_copy(h, t, x).start()
-
-            @pl.when(x == 2 * h + t)
-            def _():
-                last_a[x] = part_a[h, t]
-
-        @pl.when(mine_half == h)
-        def _():
-            @pl.loop(1, side)
-            def _(i):
-                sum_b(h, 0, x ^ i).wait_recv()
-
-            part_b[...] = jnp.sum(in_b[...], axis=0)
-            last_b[y] = part_b[y]
-
-            @pl.loop(1, side)
-            def _(i):
-                last_b_copy(i).start()
-
-    multiply(0)
-
     sums = dot(jnp.ones((8, depth), BF16), cot_all[...].reshape(depth, dm))
     for i in range(dm // 128):
         span_bias[s, i : i + 1, :] = sums[0:1, i * 128 : (i + 1) * 128]
@@ -415,7 +416,25 @@
     def _(i):
         bias_copy(i).start()
 
-    multiply(1)
+    @pl.loop(1, spans)
+    def _(i):
+        tok_copy(0, i).wait_send()
+        tok_copy(1, i).wait_send()
+        back_copy(i).wait_send()
+
+    @pl.loop(1, views)
+    def _(i):
+        blk_copy(0, i).wait_send()
+        blk_copy(1, i).wait_send()
+
+    for k in range(1, steps + 1):
+        ring_copy(0, k).wait_send()
+        ring_copy(1, k).wait_send()
+
+    @pl.loop(0, nz)
+    def _(k):
+        share_copy(k).wait_send()
+
     combine(0)
     combine(1)
 
@@ -432,6 +451,15 @@
 
     bias_grad_ref[...] = jnp.sum(span_bias[...], axis=0) * scale
     bias_put.start()
+
+    @pl.loop(1, spans)
+    def _(i):
+        bias_copy(i).wait_send()
+
+    @pl.loop(1, side)
+    def _(i):
+        sum_a(0, i).wait_send()
+        sum_a(1, i).wait_send()
 
     @pl.loop(1, side)
     def _(i):
@@ -442,30 +470,8 @@
     weight_grad_ref[:, na:] = jnp.sum(last_b[...], axis=0) * scale
     weight_put.start()
 
-    @pl.loop(1, spans)
-    def _(i):
-        tok_copy(0, i).wait_send()
-        tok_copy(1, i).wait_send()
-        back_copy(i).wait_send()
-        bias_copy(i).wait_send()
-
-    @pl.loop(1, views)
-    def _(i):
-        blk_copy(0, i).wait_send()
-        blk_copy(1, i).wait_send()
-
-    for k in range(1, steps + 1):
-        ring_copy(0, k).wait_send()
-        ring_copy(1, k).wait_send()
-
-    @pl.loop(0, nz)
-    def _(k):
-        share_copy(k).wait_send()
-
     @pl.loop(1, side)
     def _(i):
-        sum_a(0, i).wait_send()
-        sum_a(1, i).wait_send()
         last_b_copy(i).wait_send()
 
     for h in range(2):

time: 53.4 us -> 53.2 us (level)
  no operation moved by 1% of the time
where the time goes in v6:
time: 53.2 us; the launch traced here: 53 us
  Pallas kernels  52.4 us (98%)
  between operations  0.64 us (1%)
    pallas_call x1, Pallas kernels, body(): pl.pallas_call(functools.partial(kernel, views, spans, 128, scale), out_s...  50.4 us
    pallas_call x1, Pallas kernels, body(): pl.pallas_call(hand_over, out_shape=tuple((jax.ShapeDtypeStruct(r.shape,...  1.99 us

profile of v6, /device:TPU:23, one launch (start us, length us, event | category | flops | bytes accessed | tf_op | source)
XLA Modules:
  0.0 53.0 jit_solution(4826710100894112224)
XLA Ops:
  0.6 50.4 %shard_map.84 = (bf16[1,64,1024]{2,1,0:T(8,128)(2,1)}, bf16[1,256,1024]{2,1,0:T(8,128)(2,1)}, f32[16,1024]{1,0:T(8,128)}, f32[8,128]{1,0:T(8,128)}) custom-call(bf16[1,256,1024]{2,1,0:T(8,128)(2,1)} %tokens_hbm.1, s32[1,4096]{1,0:T(1,128)} %order_hbm.1, bf16[4096,1024]{1,0:T(8,128)(2,1)} %w_hbm.1, bf16[1024]{0:T(1024)(128)(2,1)} %bias_hbm.1, ...), custom_call_target="tpu_custom_call" | custom-call | tf_op jit(solution)/shard_map/pallas_call | solution.py:521
  51.0 2.0 %shard_map.85 = (bf16[1,64,1024]{2,1,0:T(8,128)(2,1)}, bf16[1,256,1024]{2,1,0:T(8,128)(2,1)}, f32[16,1024]{1,0:T(8,128)}, f32[8,128]{1,0:T(8,128)}) custom-call(bf16[1,64,1024]{2,1,0:T(8,128)(2,1)} %get-tuple-element.12.refs_0_, bf16[1,256,1024]{2,1,0:T(8,128)(2,1)} %get-tuple-element.13.refs_1_, f32[16,1024]{1,0:T(8,128)} %get-tuple-element.14.refs_2_, ...), custom_call_target="tpu_custom_call" | custom-call | tf_op jit(solution)/shard_map/pallas_call | solution.py:588

commit v7 on v6

--- a/solution.py
+++ b/solution.py
@@ -435,15 +435,15 @@
     def _(k):
         share_copy(k).wait_send()
 
+    @pl.loop(1, spans)
+    def _(i):
+        back_copy(i).wait_recv()
+
+    token_grad_ref[0] = dot(pick_ref[...], unpair(ret_ref[...]), TN).astype(BF16)
+    tokens_put.start()
+
     combine(0)
     combine(1)
-
-    @pl.loop(1, spans)
-    def _(i):
-        back_copy(i).wait_recv()
-
-    token_grad_ref[0] = dot(pick_ref[...], unpair(ret_ref[...]), TN).astype(BF16)
-    tokens_put.start()
 
     @pl.loop(1, spans)
     def _(i):

time: 53.2 us -> 53.2 us (level)
  no operation moved by 1% of the time
where the time goes in v7:
time: 53.2 us; the launch traced here: 53 us
  Pallas kernels  52.4 us (98%)
  between operations  0.64 us (1%)
    pallas_call x1, Pallas kernels, body(): pl.pallas_call(functools.partial(kernel, views, spans, 128, scale), out_s...  50.4 us
    pallas_call x1, Pallas kernels, body(): pl.pallas_call(hand_over, out_shape=tuple((jax.ShapeDtypeStruct(r.shape,...  1.99 us

profile of v7, /device:TPU:23, one launch (start us, length us, event | category | flops | bytes accessed | tf_op | source)
XLA Modules:
  0.0 53.0 jit_solution(4461148570229160430)
XLA Ops:
  0.6 50.4 %shard_map.84 = (bf16[1,64,1024]{2,1,0:T(8,128)(2,1)}, bf16[1,256,1024]{2,1,0:T(8,128)(2,1)}, f32[16,1024]{1,0:T(8,128)}, f32[8,128]{1,0:T(8,128)}) custom-call(bf16[1,256,1024]{2,1,0:T(8,128)(2,1)} %tokens_hbm.1, s32[1,4096]{1,0:T(1,128)} %order_hbm.1, bf16[4096,1024]{1,0:T(8,128)(2,1)} %w_hbm.1, bf16[1024]{0:T(1024)(128)(2,1)} %bias_hbm.1, ...), custom_call_target="tpu_custom_call" | custom-call | tf_op jit(solution)/shard_map/pallas_call | solution.py:521
  51.0 2.0 %shard_map.85 = (bf16[1,64,1024]{2,1,0:T(8,128)(2,1)}, bf16[1,256,1024]{2,1,0:T(8,128)(2,1)}, f32[16,1024]{1,0:T(8,128)}, f32[8,128]{1,0:T(8,128)}) custom-call(bf16[1,64,1024]{2,1,0:T(8,128)(2,1)} %get-tuple-element.12.refs_0_, bf16[1,256,1024]{2,1,0:T(8,128)(2,1)} %get-tuple-element.13.refs_1_, f32[16,1024]{1,0:T(8,128)} %get-tuple-element.14.refs_2_, ...), custom_call_target="tpu_custom_call" | custom-call | tf_op jit(solution)/shard_map/pallas_call | solution.py:588
